TPU v7x, 128 devices: a whole 4x4x4 slice. The times are simulated.
128 devices in a mesh: wall: 4 (over y), span: 32 (over x, z, core).
Axes of the slice: x: 4, y: 4, z: 4, core: 2. Of those that a mesh axis runs over, the one named last changes fastest.
Arguments:
- jac_lower: bfloat16 [8, 112, 112, 4096], P('wall', None, None, 'span')
- jac_inv_diag: bfloat16 [8, 112, 112, 4096], P('wall', None, None, 'span')
- jac_upper: bfloat16 [8, 112, 112, 4096], P('wall', None, None, 'span')
- residual: float32 [8, 112, 4096], P('wall', None, 'span'), may hold values from -6 to 6
- prev_update: float32 [8, 112, 4096], P('wall', None, 'span'), may hold values from -6 to 6
- send_lines: int32 [32, 32, 64], P('span'), may hold values from 0 to 127
- send_count: int32 [32, 32], P('span'), may hold values from 1 to 64, as said below
- recv_lines: int32 [32, 32, 64], P('span'), may hold values from 0 to 127
- active_lines: int32 [32], P('span'), may hold values from 64 to 128, as said below
Outputs:
- line_update: float32 [8, 112, 4096], P('wall', None, 'span')
Inputs may be any that keep to these rules, and one draw needn't show every extreme that they name: `send_count`: every sender fills all 64 slots towards at least one receiver, and one receiver gets full slots from every sender. `active_lines`: at least one device has all 128 lines live.
All inputs are finite; a program needn't handle non-finite values.
Results may differ from a plain program's by a relative error of at most 0.0003.
Values sent between devices are 32-bit elements; how exact they have to be, the bound alone decides.
A program may use at most 256 MiB of HBM per device.

v0:
```python
import jax
import jax.numpy as jnp
from jax import lax
from jax.sharding import PartitionSpec as P


def from_behind(value, axis, steps):
    count = lax.axis_size(axis)
    first, last = (max(0, -steps), min(count, count - steps))
    return lax.ppermute(value, axis, [(source, source + steps) for source in range(first, last)])


def matvec(block, vec):
    return jnp.einsum("abl,bl->al", block.astype(jnp.float32), vec, precision=lax.Precision.HIGHEST)


def lower_sweep(jac_lower, rhs, start_vec):

    def lower_step(carry, inputs):
        block, right = inputs
        value = right - matvec(block, carry)
        return (value, value)

    return lax.scan(lower_step, start_vec, (jac_lower, rhs))


def upper_sweep(jac_inv_diag, jac_upper, values, start_vec):

    def upper_step(carry, inputs):
        inverse, block, right = inputs
        value = matvec(inverse, right - matvec(block, carry))
        return (value, value)

    return lax.scan(upper_step, start_vec, (jac_inv_diag, jac_upper, values), reverse=True)


def local(
    jac_lower,
    jac_inv_diag,
    jac_upper,
    residual,
    prev_update,
    send_lines,
    send_count,
    recv_lines,
    active_lines,
):
    cells, width, _, lanes = jac_lower.shape
    spans = lax.axis_size("span")
    slot_count = send_lines.shape[2]
    lane_ids = jnp.arange(lanes, dtype=jnp.int32)
    slot_ids = jnp.arange(slot_count, dtype=jnp.int32)
    tiles = prev_update.reshape(cells * width, lanes)
    keep = (slot_ids[None, :] < send_count[0][:, None]) & (send_lines[0] < active_lines[0])
    picks = (lane_ids[:, None] == send_lines[0].reshape(-1)[None, :]) & keep.reshape(-1)[None, :]
    outgoing = jnp.dot(tiles, picks.astype(jnp.float32), precision=lax.Precision.HIGHEST)
    outgoing = outgoing.reshape(cells * width, spans, slot_count)
    incoming = lax.all_to_all(outgoing, "span", split_axis=1, concat_axis=1, tiled=True)
    landing = (recv_lines[0].reshape(-1)[:, None] == lane_ids[None, :]).astype(jnp.float32)
    coupling = jnp.dot(
        incoming.reshape(cells * width, spans * slot_count),
        landing,
        precision=lax.Precision.HIGHEST,
    )
    live = (lane_ids < active_lines[0]).astype(jnp.float32)
    rhs = (residual - coupling.reshape(cells, width, lanes)) * live[None, None, :]
    zero_vec = jnp.zeros((width, lanes), jnp.float32)
    entering = zero_vec
    for turn in range(lax.axis_size("wall") - 1):
        last, values = lower_sweep(jac_lower, rhs, entering)
        entering = from_behind(last, "wall", 1)
    last, values = lower_sweep(jac_lower, rhs, entering)
    leaving = zero_vec
    for turn in range(lax.axis_size("wall") - 1):
        first, result = upper_sweep(jac_inv_diag, jac_upper, values, leaving)
        leaving = from_behind(first, "wall", -1)
    first, result = upper_sweep(jac_inv_diag, jac_upper, values, leaving)
    return result


def solution(mesh):
    return jax.shard_map(
        local,
        mesh=mesh,
        in_specs=(
            P("wall", None, None, "span"),
            P("wall", None, None, "span"),
            P("wall", None, None, "span"),
            P("wall", None, "span"),
            P("wall", None, "span"),
            P("span", None, None),
            P("span", None),
            P("span", None, None),
            P("span"),
        ),
        out_specs=P("wall", None, "span"),
        check_vma=False,
    )
```

profile of v0, /device:TPU:16, one launch (start us, length us, event | category | flops | bytes accessed | tf_op | source)
XLA Modules:
  0.0 157.9 jit_solution(12267908807093458648)
XLA Ops:
  0.0 0.8 eq.31
  1.5 0.7 iota_compare_fusion.2
  2.2 0.1 lt.86
  2.3 0.9 convolution_bitcast_fusion
  3.2 1.8 %copy.11 = f32[224,2048]{0,1:T(8,128)} copy(f32[224,2048]{1,0:T(8,128)S(1)} %convolution_bitcast_fusion) | data formatting | bytes 3670016 | tf_op jit(solution)/shard_map/dot_general | solution.py:56
  5.1 8.3 %all-to-all-start = ((f32[224,32,64]{0,2,1:T(8,128)}), f32[224,32,64]{0,2,1:T(8,128)}, u32[]{:S(2)}, u32[]{:S(2)}) async-start(f32[224,32,64]{0,2,1:T(8,128)} %bitcast.70), calls=%async_computation | async-start | bytes 4194304 | tf_op jit(solution)/shard_map/all_to_all | solution.py:58
  13.4 28.8 %all-to-all-done = f32[224,32,64]{0,2,1:T(8,128)} async-done(((f32[224,32,64]{0,2,1:T(8,128)}), f32[224,32,64]{0,2,1:T(8,128)}, u32[]{:S(2)}, u32[]{:S(2)}) %all-to-all-start) | async-done | bytes 1835040 | tf_op jit(solution)/shard_map/all_to_all | solution.py:58
  42.3 2.6 %dot_general.72 = f32[2,112,2048]{1,0,2:T(2,128)S(1)} reshape(f32[224,32,64]{0,2,1:T(8,128)} %all-to-all-done) | data formatting | bytes 3670016 | tf_op jit(solution)/shard_map/dot_general | solution.py:60
  44.9 2.1 %fusion.9 = f32[2,112,128]{2,1,0:T(8,128)S(1)} fusion(f32[2,112,128]{2,1,0:T(8,128)S(1)} %copy-done.2, f32[2,112,2048]{1,0,2:T(2,128)S(1)} %dot_general.72, s32[2048]{0:T(1024)S(1)} %eq.34, f32[128]{0:T(128)S(1)} %compare_convert_fusion), kind=kOutput, calls=%fused_computation.31 | convolution fusion | flops 704962560 | bytes 2073088 | tf_op jit(solution)/shard_map/dot_general | solution.py:60
  47.0 6.1 %while.108 = (s32[]{:T(128)}, f32[112,128]{1,0:T(8,128)S(1)}, f32[2,112,128]{2,1,0:T(8,128)S(1)}, bf16[2,112,112,128]{3,2,1,0:T(8,128)(2,1)}, s32[]{:T(128)}, /*index=5*/s32[]{:T(128)}) while((s32[]{:T(128)}, f32[112,128]{1,0:T(8,128)S(1)}, f32[2,112,128]{2,1,0:T(8,128)S(1)}, bf16[2,112,112,128]{3,2,1,0:T(8,128)(2,1)}, s32[]{:T(128)}, ...), condition=%wide.region_1.2_spmd.clone, body=%wide.region_0.1_spmd.clone.sunk | while | flops 4831235 | bytes 3612759 | solution.py:24
  47.0 3.0 %multiply_reduce_fusion.35 = f32[128,112]{0,1:T(8,128)S(1)} fusion(f32[128,112]{0,1:T(8,128)S(1)} %select_bitcast_fusion.2, bf16[2,112,112,128]{3,2,1,0:T(8,128)(2,1)} %get-tuple-element.885, s32[]{:T(128)} %get-tuple-element.876), kind=kLoop, calls=%fused_computation.24.clone.1 | loop fusion | flops 4802560 | bytes 3325956 | tf_op jit(solution)/shard_map/while/body/eval_jaxpr/abl,bl->al/dot_general | solution.py:14
  50.1 3.0 %multiply_reduce_fusion.35 = f32[128,112]{0,1:T(8,128)S(1)} fusion(f32[128,112]{0,1:T(8,128)S(1)} %select_bitcast_fusion.2, bf16[2,112,112,128]{3,2,1,0:T(8,128)(2,1)} %get-tuple-element.885, s32[]{:T(128)} %get-tuple-element.876), kind=kLoop, calls=%fused_computation.24.clone.1 | loop fusion | flops 4802560 | bytes 3325956 | tf_op jit(solution)/shard_map/while/body/eval_jaxpr/abl,bl->al/dot_general | solution.py:14
  53.1 3.2 %collective-permute-start = (f32[112,128]{1,0:T(8,128)S(1)}, f32[112,128]{1,0:T(8,128)S(1)}, u32[]{:S(2)}, u32[]{:S(2)}) collective-permute-start(f32[112,128]{1,0:T(8,128)S(1)} %get-tuple-element.529), channel_id=1, source_target_pairs={{0,32},{32,64},{64,96},{1,33},{33,65},{65,97},{2,34},{34,66},{66,9... | collective-permute-start | bytes 172040 | tf_op jit(solution)/shard_map/ppermute | solution.py:10
  56.3 2.9 %collective-permute-done = f32[112,128]{1,0:T(8,128)S(1)} collective-permute-done((f32[112,128]{1,0:T(8,128)S(1)}, f32[112,128]{1,0:T(8,128)S(1)}, u32[]{:S(2)}, u32[]{:S(2)}) %collective-permute-start) | collective-permute-done | bytes 57376 | tf_op jit(solution)/shard_map/ppermute | solution.py:10
  59.2 6.0 %while.101 = (s32[]{:T(128)}, f32[112,128]{1,0:T(8,128)S(1)}, f32[2,112,128]{2,1,0:T(8,128)S(1)}, bf16[2,112,112,128]{3,2,1,0:T(8,128)(2,1)}, s32[]{:T(128)}) while((s32[]{:T(128)}, f32[112,128]{1,0:T(8,128)S(1)}, f32[2,112,128]{2,1,0:T(8,128)S(1)}, bf16[2,112,112,128]{3,2,1,0:T(8,128)(2,1)}, s32[]{:T(128)}) %tuple.213), condition=%wide.region_3.4_spmd, body=%wide.region_2.3_spmd.sunk | while | flops 4816898 | bytes 3498053 | solution.py:24
  59.2 3.0 %multiply_reduce_fusion.24 = f32[128,112]{0,1:T(8,128)S(1)} fusion(f32[128,112]{0,1:T(8,128)S(1)} %bitcast.228, bf16[2,112,112,128]{3,2,1,0:T(8,128)(2,1)} %get-tuple-element.901, s32[]{:T(128)} %get-tuple-element.893), kind=kLoop, calls=%fused_computation.clone.1 | loop fusion | flops 4802560 | bytes 3325956 | tf_op jit(solution)/shard_map/while/body/eval_jaxpr/abl,bl->al/dot_general | solution.py:14
  62.2 3.0 %multiply_reduce_fusion.24 = f32[128,112]{0,1:T(8,128)S(1)} fusion(f32[128,112]{0,1:T(8,128)S(1)} %bitcast.228, bf16[2,112,112,128]{3,2,1,0:T(8,128)(2,1)} %get-tuple-element.901, s32[]{:T(128)} %get-tuple-element.893), kind=kLoop, calls=%fused_computation.clone.1 | loop fusion | flops 4802560 | bytes 3325956 | tf_op jit(solution)/shard_map/while/body/eval_jaxpr/abl,bl->al/dot_general | solution.py:14
  65.2 3.2 %collective-permute-start.1 = (f32[112,128]{1,0:T(8,128)S(1)}, f32[112,128]{1,0:T(8,128)S(1)}, u32[]{:S(2)}, u32[]{:S(2)}) collective-permute-start(f32[112,128]{1,0:T(8,128)S(1)} %get-tuple-element.530), channel_id=1, source_target_pairs={{0,32},{32,64},{64,96},{1,33},{33,65},{65,97},{2,34},{34,66},{66,9... | collective-permute-start | bytes 172040 | tf_op jit(solution)/shard_map/ppermute | solution.py:10
  68.4 2.9 %collective-permute-done.1 = f32[112,128]{1,0:T(8,128)S(1)} collective-permute-done((f32[112,128]{1,0:T(8,128)S(1)}, f32[112,128]{1,0:T(8,128)S(1)}, u32[]{:S(2)}, u32[]{:S(2)}) %collective-permute-start.1) | collective-permute-done | bytes 57376 | tf_op jit(solution)/shard_map/ppermute | solution.py:10
  71.3 6.0 %while.102 = (s32[]{:T(128)}, f32[112,128]{1,0:T(8,128)S(1)}, f32[2,112,128]{2,1,0:T(8,128)S(1)}, bf16[2,112,112,128]{3,2,1,0:T(8,128)(2,1)}, s32[]{:T(128)}) while((s32[]{:T(128)}, f32[112,128]{1,0:T(8,128)S(1)}, f32[2,112,128]{2,1,0:T(8,128)S(1)}, bf16[2,112,112,128]{3,2,1,0:T(8,128)(2,1)}, s32[]{:T(128)}) %tuple.214), condition=%wide.region_5.6_spmd, body=%wide.region_4.5_spmd.sunk | while | flops 4816898 | bytes 3498053 | solution.py:24
  71.3 3.0 %multiply_reduce_fusion.25 = f32[128,112]{0,1:T(8,128)S(1)} fusion(f32[128,112]{0,1:T(8,128)S(1)} %bitcast.229, bf16[2,112,112,128]{3,2,1,0:T(8,128)(2,1)} %get-tuple-element.916, s32[]{:T(128)} %get-tuple-element.908), kind=kLoop, calls=%fused_computation.2.clone.1 | loop fusion | flops 4802560 | bytes 3325956 | tf_op jit(solution)/shard_map/while/body/eval_jaxpr/abl,bl->al/dot_general | solution.py:14
  74.3 3.0 %multiply_reduce_fusion.25 = f32[128,112]{0,1:T(8,128)S(1)} fusion(f32[128,112]{0,1:T(8,128)S(1)} %bitcast.229, bf16[2,112,112,128]{3,2,1,0:T(8,128)(2,1)} %get-tuple-element.916, s32[]{:T(128)} %get-tuple-element.908), kind=kLoop, calls=%fused_computation.2.clone.1 | loop fusion | flops 4802560 | bytes 3325956 | tf_op jit(solution)/shard_map/while/body/eval_jaxpr/abl,bl->al/dot_general | solution.py:14
  77.3 3.2 %collective-permute-start.2 = (f32[112,128]{1,0:T(8,128)S(1)}, f32[112,128]{1,0:T(8,128)S(1)}, u32[]{:S(2)}, u32[]{:S(2)}) collective-permute-start(f32[112,128]{1,0:T(8,128)S(1)} %get-tuple-element.531), channel_id=1, source_target_pairs={{0,32},{32,64},{64,96},{1,33},{33,65},{65,97},{2,34},{34,66},{66,9... | collective-permute-start | bytes 172040 | tf_op jit(solution)/shard_map/ppermute | solution.py:10
  80.5 2.9 %collective-permute-done.2 = f32[112,128]{1,0:T(8,128)S(1)} collective-permute-done((f32[112,128]{1,0:T(8,128)S(1)}, f32[112,128]{1,0:T(8,128)S(1)}, u32[]{:S(2)}, u32[]{:S(2)}) %collective-permute-start.2) | collective-permute-done | bytes 57376 | tf_op jit(solution)/shard_map/ppermute | solution.py:10
  83.4 6.1 %while.103 = (s32[]{:T(128)}, f32[112,128]{1,0:T(8,128)S(1)}, f32[2,112,128]{2,1,0:T(8,128)S(1)}, f32[2,112,128]{2,1,0:T(8,128)S(1)}, bf16[2,112,112,128]{3,2,1,0:T(8,128)(2,1)}, /*index=5*/s32[]{:T(128)}) while((s32[]{:T(128)}, f32[112,128]{1,0:T(8,128)S(1)}, f32[2,112,128]{2,1,0:T(8,128)S(1)}, f32[2,112,128]{2,1,0:T(8,128)S(1)}, ...), condition=%wide.region_7.8_spmd, body=%wide.region_6.7_spmd.sunk | while | flops 4816898 | bytes 3555405 | solution.py:24
  83.4 3.0 %multiply_reduce_fusion.26 = f32[128,112]{0,1:T(8,128)S(1)} fusion(f32[128,112]{0,1:T(8,128)S(1)} %bitcast.227, bf16[2,112,112,128]{3,2,1,0:T(8,128)(2,1)} %get-tuple-element.934, s32[]{:T(128)} %get-tuple-element.924), kind=kLoop, calls=%fused_computation.4.clone.1 | loop fusion | flops 4802560 | bytes 3325956 | tf_op jit(solution)/shard_map/while/body/eval_jaxpr/abl,bl->al/dot_general | solution.py:14
  86.5 3.0 %multiply_reduce_fusion.26 = f32[128,112]{0,1:T(8,128)S(1)} fusion(f32[128,112]{0,1:T(8,128)S(1)} %bitcast.227, bf16[2,112,112,128]{3,2,1,0:T(8,128)(2,1)} %get-tuple-element.934, s32[]{:T(128)} %get-tuple-element.924), kind=kLoop, calls=%fused_computation.4.clone.1 | loop fusion | flops 4802560 | bytes 3325956 | tf_op jit(solution)/shard_map/while/body/eval_jaxpr/abl,bl->al/dot_general | solution.py:14
  89.5 12.4 %while.104 = (s32[]{:T(128)}, f32[112,128]{0,1:T(8,128)S(1)}, f32[2,112,128]{2,1,0:T(8,128)S(1)}, bf16[2,112,112,128]{3,2,1,0:T(8,128)(2,1)}, bf16[2,112,112,128]{3,2,1,0:T(8,128)(2,1)}, /*index=5*/s32[]{:T(128)}) while((s32[]{:T(128)}, f32[112,128]{0,1:T(8,128)S(1)}, f32[2,112,128]{2,1,0:T(8,128)S(1)}, bf16[2,112,112,128]{3,2,1,0:T(8,128)(2,1)}, ...), condition=%wide.region_9.10_spmd, body=%wide.region_8.9_spmd.sunk | while | flops 9619459 | bytes 7053405 | solution.py:34
  89.5 0.1 copy.119
  89.6 3.0 %multiply_reduce_fusion.27 = f32[128,112]{0,1:T(8,128)S(1)} fusion(f32[128,112]{0,1:T(8,128)S(1)} %copy.119, bf16[2,112,112,128]{3,2,1,0:T(8,128)(2,1)} %get-tuple-element.951, s32[]{:T(128)S(6)} %sub.115), kind=kLoop, calls=%fused_computation.8.clone.1 | loop fusion | flops 4802560 | bytes 3325956 | tf_op jit(solution)/shard_map/while/body/eval_jaxpr/abl,bl->al/dot_general | solution.py:14
  92.6 3.0 %multiply_reduce_fusion.28 = f32[128,112]{0,1:T(8,128)S(1)} fusion(f32[128,112]{0,1:T(8,128)S(1)} %fusion.24, bf16[2,112,112,128]{3,2,1,0:T(8,128)(2,1)} %get-tuple-element.952, s32[]{:T(128)S(6)} %sub.115), kind=kLoop, calls=%fused_computation.7.clone.1 | loop fusion | flops 4802560 | bytes 3325956 | tf_op jit(solution)/shard_map/while
  95.6 0.1 copy.120
  95.7 0.1 copy.119
  95.8 3.0 %multiply_reduce_fusion.27 = f32[128,112]{0,1:T(8,128)S(1)} fusion(f32[128,112]{0,1:T(8,128)S(1)} %copy.119, bf16[2,112,112,128]{3,2,1,0:T(8,128)(2,1)} %get-tuple-element.951, s32[]{:T(128)S(6)} %sub.115), kind=kLoop, calls=%fused_computation.8.clone.1 | loop fusion | flops 4802560 | bytes 3325956 | tf_op jit(solution)/shard_map/while/body/eval_jaxpr/abl,bl->al/dot_general | solution.py:14
  98.8 3.0 %multiply_reduce_fusion.28 = f32[128,112]{0,1:T(8,128)S(1)} fusion(f32[128,112]{0,1:T(8,128)S(1)} %fusion.24, bf16[2,112,112,128]{3,2,1,0:T(8,128)(2,1)} %get-tuple-element.952, s32[]{:T(128)S(6)} %sub.115), kind=kLoop, calls=%fused_computation.7.clone.1 | loop fusion | flops 4802560 | bytes 3325956 | tf_op jit(solution)/shard_map/while
  101.8 0.1 copy.120
  101.9 2.5 %collective-permute-start.3 = (f32[112,128]{0,1:T(8,128)S(1)}, f32[112,128]{0,1:T(8,128)S(1)}, u32[]{:S(2)}, u32[]{:S(2)}) collective-permute-start(f32[112,128]{0,1:T(8,128)S(1)} %get-tuple-element.533), channel_id=1, source_target_pairs={{32,0},{64,32},{96,64},{33,1},{65,33},{97,65},{34,2},{66,34},{98,6... | collective-permute-start | bytes 172040 | tf_op jit(solution)/shard_map/ppermute | solution.py:10
  104.5 3.6 %collective-permute-done.3 = f32[112,128]{0,1:T(8,128)S(1)} collective-permute-done((f32[112,128]{0,1:T(8,128)S(1)}, f32[112,128]{0,1:T(8,128)S(1)}, u32[]{:S(2)}, u32[]{:S(2)}) %collective-permute-start.3) | collective-permute-done | bytes 57376 | tf_op jit(solution)/shard_map/ppermute | solution.py:10
  108.1 12.4 %while.105 = (s32[]{:T(128)}, f32[112,128]{0,1:T(8,128)S(1)}, f32[2,112,128]{2,1,0:T(8,128)S(1)}, bf16[2,112,112,128]{3,2,1,0:T(8,128)(2,1)}, bf16[2,112,112,128]{3,2,1,0:T(8,128)(2,1)}, /*index=5*/s32[]{:T(128)}) while((s32[]{:T(128)}, f32[112,128]{0,1:T(8,128)S(1)}, f32[2,112,128]{2,1,0:T(8,128)S(1)}, ...), condition=%wide.region_11.12_spmd, body=%wide.region_10.11_spmd.sunk | while | flops 9619459 | bytes 7053405 | solution.py:34
  108.2 3.0 %multiply_reduce_fusion.29 = f32[128,112]{0,1:T(8,128)S(1)} fusion(f32[128,112]{0,1:T(8,128)S(1)} %copy.121, bf16[2,112,112,128]{3,2,1,0:T(8,128)(2,1)} %get-tuple-element.969, s32[]{:T(128)S(6)} %sub.117), kind=kLoop, calls=%fused_computation.12.clone.1 | loop fusion | flops 4802560 | bytes 3325956 | tf_op jit(solution)/shard_map/while/body/eval_jaxpr/abl,bl->al/dot_general | solution.py:14
  111.2 3.0 %multiply_reduce_fusion.30 = f32[128,112]{0,1:T(8,128)S(1)} fusion(f32[128,112]{0,1:T(8,128)S(1)} %fusion.25, bf16[2,112,112,128]{3,2,1,0:T(8,128)(2,1)} %get-tuple-element.970, s32[]{:T(128)S(6)} %sub.117), kind=kLoop, calls=%fused_computation.11.clone.1 | loop fusion | flops 4802560 | bytes 3325956 | tf_op jit(solution)/shard_map/while
  114.2 0.1 copy.122
  114.3 0.1 copy.121
  114.4 3.0 %multiply_reduce_fusion.29 = f32[128,112]{0,1:T(8,128)S(1)} fusion(f32[128,112]{0,1:T(8,128)S(1)} %copy.121, bf16[2,112,112,128]{3,2,1,0:T(8,128)(2,1)} %get-tuple-element.969, s32[]{:T(128)S(6)} %sub.117), kind=kLoop, calls=%fused_computation.12.clone.1 | loop fusion | flops 4802560 | bytes 3325956 | tf_op jit(solution)/shard_map/while/body/eval_jaxpr/abl,bl->al/dot_general | solution.py:14
  117.4 3.0 %multiply_reduce_fusion.30 = f32[128,112]{0,1:T(8,128)S(1)} fusion(f32[128,112]{0,1:T(8,128)S(1)} %fusion.25, bf16[2,112,112,128]{3,2,1,0:T(8,128)(2,1)} %get-tuple-element.970, s32[]{:T(128)S(6)} %sub.117), kind=kLoop, calls=%fused_computation.11.clone.1 | loop fusion | flops 4802560 | bytes 3325956 | tf_op jit(solution)/shard_map/while
  120.4 0.1 copy.122
  120.5 2.4 %collective-permute-start.4 = (f32[112,128]{0,1:T(8,128)S(1)}, f32[112,128]{0,1:T(8,128)S(1)}, u32[]{:S(2)}, u32[]{:S(2)}) collective-permute-start(f32[112,128]{0,1:T(8,128)S(1)} %get-tuple-element.534), channel_id=1, source_target_pairs={{32,0},{64,32},{96,64},{33,1},{65,33},{97,65},{34,2},{66,34},{98,6... | collective-permute-start | bytes 172040 | tf_op jit(solution)/shard_map/ppermute | solution.py:10
  122.8 3.8 %collective-permute-done.4 = f32[112,128]{0,1:T(8,128)S(1)} collective-permute-done((f32[112,128]{0,1:T(8,128)S(1)}, f32[112,128]{0,1:T(8,128)S(1)}, u32[]{:S(2)}, u32[]{:S(2)}) %collective-permute-start.4) | collective-permute-done | bytes 57376 | tf_op jit(solution)/shard_map/ppermute | solution.py:10
  126.6 12.4 %while.106 = (s32[]{:T(128)}, f32[112,128]{0,1:T(8,128)S(1)}, f32[2,112,128]{2,1,0:T(8,128)S(1)}, bf16[2,112,112,128]{3,2,1,0:T(8,128)(2,1)}, bf16[2,112,112,128]{3,2,1,0:T(8,128)(2,1)}, /*index=5*/s32[]{:T(128)}) while((s32[]{:T(128)}, f32[112,128]{0,1:T(8,128)S(1)}, f32[2,112,128]{2,1,0:T(8,128)S(1)}, ...), condition=%wide.region_13.14_spmd, body=%wide.region_12.13_spmd.sunk | while | flops 9619459 | bytes 7053405 | solution.py:34
  126.7 3.0 %multiply_reduce_fusion.31 = f32[128,112]{0,1:T(8,128)S(1)} fusion(f32[128,112]{0,1:T(8,128)S(1)} %copy.123, bf16[2,112,112,128]{3,2,1,0:T(8,128)(2,1)} %get-tuple-element.987, s32[]{:T(128)S(6)} %sub.119), kind=kLoop, calls=%fused_computation.16.clone.1 | loop fusion | flops 4802560 | bytes 3325956 | tf_op jit(solution)/shard_map/while/body/eval_jaxpr/abl,bl->al/dot_general | solution.py:14
  129.7 3.0 %multiply_reduce_fusion.32 = f32[128,112]{0,1:T(8,128)S(1)} fusion(f32[128,112]{0,1:T(8,128)S(1)} %fusion.26, bf16[2,112,112,128]{3,2,1,0:T(8,128)(2,1)} %get-tuple-element.988, s32[]{:T(128)S(6)} %sub.119), kind=kLoop, calls=%fused_computation.15.clone.1 | loop fusion | flops 4802560 | bytes 3325956 | tf_op jit(solution)/shard_map/while
  132.7 0.1 copy.124
  132.8 0.1 copy.123
  132.9 3.0 %multiply_reduce_fusion.31 = f32[128,112]{0,1:T(8,128)S(1)} fusion(f32[128,112]{0,1:T(8,128)S(1)} %copy.123, bf16[2,112,112,128]{3,2,1,0:T(8,128)(2,1)} %get-tuple-element.987, s32[]{:T(128)S(6)} %sub.119), kind=kLoop, calls=%fused_computation.16.clone.1 | loop fusion | flops 4802560 | bytes 3325956 | tf_op jit(solution)/shard_map/while/body/eval_jaxpr/abl,bl->al/dot_general | solution.py:14
  135.9 3.0 %multiply_reduce_fusion.32 = f32[128,112]{0,1:T(8,128)S(1)} fusion(f32[128,112]{0,1:T(8,128)S(1)} %fusion.26, bf16[2,112,112,128]{3,2,1,0:T(8,128)(2,1)} %get-tuple-element.988, s32[]{:T(128)S(6)} %sub.119), kind=kLoop, calls=%fused_computation.15.clone.1 | loop fusion | flops 4802560 | bytes 3325956 | tf_op jit(solution)/shard_map/while
  138.9 0.1 copy.124
  139.1 2.4 %collective-permute-start.5 = (f32[112,128]{1,0:T(8,128)S(1)}, f32[112,128]{1,0:T(8,128)S(1)}, u32[]{:S(2)}, u32[]{:S(2)}) collective-permute-start(f32[112,128]{1,0:T(8,128)S(1)} %copy.13), channel_id=1, source_target_pairs={{32,0},{64,32},{96,64},{33,1},{65,33},{97,65},{34,2},{66,34},{98,6... | collective-permute-start | bytes 172040 | tf_op jit(solution)/shard_map/ppermute | solution.py:10
  141.5 3.7 %collective-permute-done.5 = f32[112,128]{1,0:T(8,128)S(1)} collective-permute-done((f32[112,128]{1,0:T(8,128)S(1)}, f32[112,128]{1,0:T(8,128)S(1)}, u32[]{:S(2)}, u32[]{:S(2)}) %collective-permute-start.5) | collective-permute-done | bytes 57376 | tf_op jit(solution)/shard_map/ppermute | solution.py:10
  145.2 12.1 %while.107 = (s32[]{:T(128)}, f32[112,128]{1,0:T(8,128)S(1)}, f32[2,112,128]{2,1,0:T(8,128)S(1)}, f32[2,112,128]{2,1,0:T(8,128)S(1)}, bf16[2,112,112,128]{3,2,1,...) while((s32[]{:T(128)}, f32[112,128]{1,0:T(8,128)S(1)}, f32[2,112,128]{2,1,0:T(8,128)S(1)}, ...), condition=%wide.region_15.16_spmd, body=%wide.region_14.15_spmd.sunk | while | flops 9619459 | bytes 6938729 | solution.py:34
  145.2 3.0 %multiply_reduce_fusion.33 = f32[128,112]{0,1:T(8,128)S(1)} fusion(f32[128,112]{0,1:T(8,128)S(1)} %bitcast.219, bf16[2,112,112,128]{3,2,1,0:T(8,128)(2,1)} %get-tuple-element.1008, s32[]{:T(128)S(6)} %sub.121), kind=kLoop, calls=%fused_computation.20.clone.1 | loop fusion | flops 4802560 | bytes 3325956 | tf_op jit(solution)/shard_map/while/body/eval_jaxpr/abl,bl->al/dot_general | solution.py:14
  148.2 3.0 %multiply_reduce_fusion.34 = f32[128,112]{0,1:T(8,128)S(1)} fusion(f32[128,112]{0,1:T(8,128)S(1)} %fusion.27, bf16[2,112,112,128]{3,2,1,0:T(8,128)(2,1)} %get-tuple-element.1009, s32[]{:T(128)S(6)} %sub.121), kind=kLoop, calls=%fused_computation.19.clone.1 | loop fusion | flops 4802560 | bytes 3325956 | tf_op jit(solution)/shard_map/while/body/eval_jaxpr/abl,bl->al/dot_general | solution.py:14
  151.3 3.0 %multiply_reduce_fusion.33 = f32[128,112]{0,1:T(8,128)S(1)} fusion(f32[128,112]{0,1:T(8,128)S(1)} %bitcast.219, bf16[2,112,112,128]{3,2,1,0:T(8,128)(2,1)} %get-tuple-element.1008, s32[]{:T(128)S(6)} %sub.121), kind=kLoop, calls=%fused_computation.20.clone.1 | loop fusion | flops 4802560 | bytes 3325956 | tf_op jit(solution)/shard_map/while/body/eval_jaxpr/abl,bl->al/dot_general | solution.py:14
  154.3 3.0 %multiply_reduce_fusion.34 = f32[128,112]{0,1:T(8,128)S(1)} fusion(f32[128,112]{0,1:T(8,128)S(1)} %fusion.27, bf16[2,112,112,128]{3,2,1,0:T(8,128)(2,1)} %get-tuple-element.1009, s32[]{:T(128)S(6)} %sub.121), kind=kLoop, calls=%fused_computation.19.clone.1 | loop fusion | flops 4802560 | bytes 3325956 | tf_op jit(solution)/shard_map/while/body/eval_jaxpr/abl,bl->al/dot_general | solution.py:14
  157.3 0.6 copy-done.1
  (37 shorter events, 0.7 us)
Async XLA Ops:
  0.0 2.3 %copy-start = (f32[2,112,128]{2,1,0:T(8,128)S(1)}, f32[2,112,128]{2,1,0:T(8,128)}, u32[]{:S(2)}) copy-start(f32[2,112,128]{2,1,0:T(8,128)} %param.29) | copy-start | bytes 344068
  0.0 13.4 %copy-start.3 = (s32[1,32,64]{2,1,0:T(8,128)S(1)}, s32[1,32,64]{2,1,0:T(8,128)}, u32[]{:S(2)}) copy-start(s32[1,32,64]{2,1,0:T(8,128)} %param.32) | copy-start | bytes 24580
  3.2 41.7 %copy-start.2 = (f32[2,112,128]{2,1,0:T(8,128)S(1)}, f32[2,112,128]{2,1,0:T(8,128)}, u32[]{:S(2)}) copy-start(f32[2,112,128]{2,1,0:T(8,128)} %param.28) | copy-start | bytes 344068
  5.1 37.2 %all-to-all-start = ((f32[224,32,64]{0,2,1:T(8,128)}), f32[224,32,64]{0,2,1:T(8,128)}, u32[]{:S(2)}, u32[]{:S(2)}) async-start(f32[224,32,64]{0,2,1:T(8,128)} %bitcast.70), calls=%async_computation | async-start | bytes 4194304 | tf_op jit(solution)/shard_map/all_to_all | solution.py:58
  53.1 6.1 %collective-permute-start = (f32[112,128]{1,0:T(8,128)S(1)}, f32[112,128]{1,0:T(8,128)S(1)}, u32[]{:S(2)}, u32[]{:S(2)}) collective-permute-start(f32[112,128]{1,0:T(8,128)S(1)} %get-tuple-element.529), channel_id=1, source_target_pairs={{0,32},{32,64},{64,96},{1,33},{33,65},{65,97},{2,34},{34,66},{66,9... | collective-permute-start | bytes 172040 | tf_op jit(solution)/shard_map/ppermute | solution.py:10
  65.2 6.1 %collective-permute-start.1 = (f32[112,128]{1,0:T(8,128)S(1)}, f32[112,128]{1,0:T(8,128)S(1)}, u32[]{:S(2)}, u32[]{:S(2)}) collective-permute-start(f32[112,128]{1,0:T(8,128)S(1)} %get-tuple-element.530), channel_id=1, source_target_pairs={{0,32},{32,64},{64,96},{1,33},{33,65},{65,97},{2,34},{34,66},{66,9... | collective-permute-start | bytes 172040 | tf_op jit(solution)/shard_map/ppermute | solution.py:10
  77.3 6.1 %collective-permute-start.2 = (f32[112,128]{1,0:T(8,128)S(1)}, f32[112,128]{1,0:T(8,128)S(1)}, u32[]{:S(2)}, u32[]{:S(2)}) collective-permute-start(f32[112,128]{1,0:T(8,128)S(1)} %get-tuple-element.531), channel_id=1, source_target_pairs={{0,32},{32,64},{64,96},{1,33},{33,65},{65,97},{2,34},{34,66},{66,9... | collective-permute-start | bytes 172040 | tf_op jit(solution)/shard_map/ppermute | solution.py:10
  101.9 6.2 %collective-permute-start.3 = (f32[112,128]{0,1:T(8,128)S(1)}, f32[112,128]{0,1:T(8,128)S(1)}, u32[]{:S(2)}, u32[]{:S(2)}) collective-permute-start(f32[112,128]{0,1:T(8,128)S(1)} %get-tuple-element.533), channel_id=1, source_target_pairs={{32,0},{64,32},{96,64},{33,1},{65,33},{97,65},{34,2},{66,34},{98,6... | collective-permute-start | bytes 172040 | tf_op jit(solution)/shard_map/ppermute | solution.py:10
  120.5 6.2 %collective-permute-start.4 = (f32[112,128]{0,1:T(8,128)S(1)}, f32[112,128]{0,1:T(8,128)S(1)}, u32[]{:S(2)}, u32[]{:S(2)}) collective-permute-start(f32[112,128]{0,1:T(8,128)S(1)} %get-tuple-element.534), channel_id=1, source_target_pairs={{32,0},{64,32},{96,64},{33,1},{65,33},{97,65},{34,2},{66,34},{98,6... | collective-permute-start | bytes 172040 | tf_op jit(solution)/shard_map/ppermute | solution.py:10
  139.1 6.1 %collective-permute-start.5 = (f32[112,128]{1,0:T(8,128)S(1)}, f32[112,128]{1,0:T(8,128)S(1)}, u32[]{:S(2)}, u32[]{:S(2)}) collective-permute-start(f32[112,128]{1,0:T(8,128)S(1)} %copy.13), channel_id=1, source_target_pairs={{32,0},{64,32},{96,64},{33,1},{65,33},{97,65},{34,2},{66,34},{98,6... | collective-permute-start | bytes 172040 | tf_op jit(solution)/shard_map/ppermute | solution.py:10
  157.3 0.6 copy-start.1
where the time goes:
time: 159 us; the launch traced here: 158 us
  other arithmetic  72.7 us (46%)
  waiting for transfers between devices  48.5 us (31%)
  starting transfers between devices  25.1 us (16%)
  local copies, waits for them, and re-layouts  7.23 us (5%)
  matrix products  3 us (2%)
    dot_general x18, other arithmetic, matvec(): jnp.einsum('abl,bl->al', block.astype(jnp.float32), vec, precision=lax.Pr...  53.7 us
    all_to_all x1, waiting for transfers between devices, local(): lax.all_to_all(outgoing, 'span', split_axis=1, concat_axis=1, tiled=True)  28.8 us
    ppermute x6, waiting for transfers between devices, from_behind(): lax.ppermute(value, axis, [(source, source + steps) for source in range(f...  19.7 us
    while x16, other arithmetic  18 us
    ppermute x6, starting transfers between devices, from_behind(): lax.ppermute(value, axis, [(source, source + steps) for source in range(f...  16.8 us
    all_to_all x1, starting transfers between devices, local(): lax.all_to_all(outgoing, 'span', split_axis=1, concat_axis=1, tiled=True)  8.29 us
  transfers between devices with their start and end apart: 7, of which 7 were waited for; matrix products, arithmetic and copies ran while one was open for 0% of the time, Pallas kernels for 0%

commit v1 on v0

--- a/solution.py
+++ b/solution.py
@@ -2,6 +2,13 @@
 import jax.numpy as jnp
 from jax import lax
 from jax.sharding import PartitionSpec as P
+
+
+def trade_parts(x, mesh_axis, split, join):
+    size = lax.axis_size(mesh_axis)
+    pieces = jnp.stack(jnp.split(x, size, axis=split), axis=0)
+    pieces = lax.all_to_all(pieces, mesh_axis, split_axis=0, concat_axis=0)
+    return jnp.concatenate(pieces, axis=join)
 
 
 def from_behind(value, axis, steps):
@@ -55,7 +62,7 @@
     picks = (lane_ids[:, None] == send_lines[0].reshape(-1)[None, :]) & keep.reshape(-1)[None, :]
     outgoing = jnp.dot(tiles, picks.astype(jnp.float32), precision=lax.Precision.HIGHEST)
     outgoing = outgoing.reshape(cells * width, spans, slot_count)
-    incoming = lax.all_to_all(outgoing, "span", split_axis=1, concat_axis=1, tiled=True)
+    incoming = trade_parts(outgoing, "span", 1, 1)
     landing = (recv_lines[0].reshape(-1)[:, None] == lane_ids[None, :]).astype(jnp.float32)
     coupling = jnp.dot(
         incoming.reshape(cells * width, spans * slot_count),

time: 159 us -> 182 us (1.14)
  local copies, waits for them, and re-layouts: 7.23 us -> 28.6 us
    unnamed x8 -> x41, local copies, waits for them, and re-layouts: 0.65 us -> 21.3 us
where the time goes in v1:
time: 182 us; the launch traced here: 181 us
  other arithmetic  72.7 us (40%)
  waiting for transfers between devices  48.6 us (27%)
  local copies, waits for them, and re-layouts  28.6 us (16%)
  starting transfers between devices  25.1 us (14%)
  matrix products  4.26 us (2%)
    dot_general x18, other arithmetic, matvec(): jnp.einsum('abl,bl->al', block.astype(jnp.float32), vec, precision=lax.Pr...  53.7 us
    all_to_all x1, waiting for transfers between devices, trade_parts(): pieces = lax.all_to_all(pieces, mesh_axis, split_axis=0, concat_axis=0)  28.8 us
    unnamed x41, local copies, waits for them, and re-layouts  21.3 us
    ppermute x6, waiting for transfers between devices, from_behind(): lax.ppermute(value, axis, [(source, source + steps) for source in range(f...  19.7 us
    while x16, other arithmetic  18 us
    ppermute x6, starting transfers between devices, from_behind(): lax.ppermute(value, axis, [(source, source + steps) for source in range(f...  16.8 us
    all_to_all x1, starting transfers between devices, trade_parts(): pieces = lax.all_to_all(pieces, mesh_axis, split_axis=0, concat_axis=0)  8.3 us
  transfers between devices with their start and end apart: 7, of which 7 were waited for; matrix products, arithmetic and copies ran while one was open for 0% of the time, Pallas kernels for 0%

profile of v1, /device:TPU:16, one launch (start us, length us, event | category | flops | bytes accessed | tf_op | source)
XLA Modules:
  0.0 180.6 jit_solution(16864981496432383237)
XLA Ops:
  0.0 0.8 eq.31
  1.5 0.7 iota_compare_fusion.2
  2.3 2.2 %convolution_bitcast_fusion = f32[224,2048]{1,0:T(8,128)} fusion(f32[224,128]{1,0:T(8,128)S(1)} %bitcast.349, s32[2048]{0:T(1024)S(1)} %eq.31, pred[2048]{0:T(1024)(128)(4,1)S(1)} %compare_and_fusion), kind=kOutput, calls=%fused_computation.27 | convolution fusion | flops 705167360 | bytes 1959936 | tf_op jit(solution)/shard_map/dot_general | solution.py:63
  4.5 1.9 %copy.43 = f32[224,2048]{0,1:T(8,128)S(1)} copy(f32[224,2048]{1,0:T(8,128)} %convolution_bitcast_fusion) | data formatting | bytes 3670016 | tf_op jit(solution)/shard_map/dot_general | solution.py:63
  6.4 0.6 constant_dynamic-update-slice_fusion.31
  9.5 0.6 constant_dynamic-update-slice_fusion.26
  11.4 0.6 constant_dynamic-update-slice_fusion.23
  15.1 0.6 constant_dynamic-update-slice_fusion.17
  15.7 0.6 constant_dynamic-update-slice_fusion.16
  21.9 0.6 constant_dynamic-update-slice_fusion.6
  23.2 0.6 constant_dynamic-update-slice_fusion.4
  23.8 0.6 constant_dynamic-update-slice_fusion.3
  25.1 0.6 constant_dynamic-update-slice_fusion.1
  25.7 0.6 constant_dynamic-update-slice_fusion
  26.3 8.3 %all-to-all-start = ((f32[32,224,1,64]{1,3,2,0:T(8,128)}), f32[32,224,1,64]{1,3,2,0:T(8,128)S(1)}, u32[]{:S(2)}, u32[]{:S(2)}) async-start(f32[32,224,1,64]{1,3,2,0:T(8,128)} %constant_dynamic-update-slice_fusion), calls=%async_computation | async-start | bytes 4194304 | tf_op jit(solution)/shard_map/all_to_all | solution.py:10
  34.7 28.8 %all-to-all-done = f32[32,224,1,64]{1,3,2,0:T(8,128)S(1)} async-done(((f32[32,224,1,64]{1,3,2,0:T(8,128)}), f32[32,224,1,64]{1,3,2,0:T(8,128)S(1)}, u32[]{:S(2)}, u32[]{:S(2)}) %all-to-all-start) | async-done | bytes 1835040 | tf_op jit(solution)/shard_map/all_to_all | solution.py:10
  63.5 1.3 copy-done.1
  64.9 2.7 %dot_general.72 = f32[2,112,2048]{1,0,2:T(2,128)S(1)} reshape(f32[224,32,1,64]{0,3,2,1:T(8,128)} %bitcast.382) | data formatting | bytes 3670016 | tf_op jit(solution)/shard_map/dot_general | solution.py:67
  67.6 2.1 %fusion.9 = f32[2,112,128]{2,1,0:T(8,128)S(1)} fusion(f32[2,112,128]{2,1,0:T(8,128)S(1)} %copy-done.3, f32[2,112,2048]{1,0,2:T(2,128)S(1)} %dot_general.72, s32[2048]{0:T(1024)S(1)} %eq.34, f32[128]{0:T(128)S(1)} %compare_convert_fusion), kind=kOutput, calls=%fused_computation.31 | convolution fusion | flops 704962560 | bytes 2073088 | tf_op jit(solution)/shard_map/dot_general | solution.py:67
  69.7 6.1 %while.108 = (s32[]{:T(128)}, f32[112,128]{1,0:T(8,128)S(1)}, f32[2,112,128]{2,1,0:T(8,128)S(1)}, bf16[2,112,112,128]{3,2,1,0:T(8,128)(2,1)}, s32[]{:T(128)}, /*index=5*/s32[]{:T(128)}) while((s32[]{:T(128)}, f32[112,128]{1,0:T(8,128)S(1)}, f32[2,112,128]{2,1,0:T(8,128)S(1)}, bf16[2,112,112,128]{3,2,1,0:T(8,128)(2,1)}, s32[]{:T(128)}, ...), condition=%wide.region_1.2_spmd.clone, body=%wide.region_0.1_spmd.clone.sunk | while | flops 4831235 | bytes 3612759 | solution.py:31
  69.7 3.0 %multiply_reduce_fusion.35 = f32[128,112]{0,1:T(8,128)S(1)} fusion(f32[128,112]{0,1:T(8,128)S(1)} %select_bitcast_fusion.2, bf16[2,112,112,128]{3,2,1,0:T(8,128)(2,1)} %get-tuple-element.885, s32[]{:T(128)} %get-tuple-element.876), kind=kLoop, calls=%fused_computation.24.clone.1 | loop fusion | flops 4802560 | bytes 3325956 | tf_op jit(solution)/shard_map/while/body/eval_jaxpr/abl,bl->al/dot_general | solution.py:21
  72.8 3.0 %multiply_reduce_fusion.35 = f32[128,112]{0,1:T(8,128)S(1)} fusion(f32[128,112]{0,1:T(8,128)S(1)} %select_bitcast_fusion.2, bf16[2,112,112,128]{3,2,1,0:T(8,128)(2,1)} %get-tuple-element.885, s32[]{:T(128)} %get-tuple-element.876), kind=kLoop, calls=%fused_computation.24.clone.1 | loop fusion | flops 4802560 | bytes 3325956 | tf_op jit(solution)/shard_map/while/body/eval_jaxpr/abl,bl->al/dot_general | solution.py:21
  75.8 3.2 %collective-permute-start = (f32[112,128]{1,0:T(8,128)S(1)}, f32[112,128]{1,0:T(8,128)S(1)}, u32[]{:S(2)}, u32[]{:S(2)}) collective-permute-start(f32[112,128]{1,0:T(8,128)S(1)} %get-tuple-element.529), channel_id=1, source_target_pairs={{0,32},{32,64},{64,96},{1,33},{33,65},{65,97},{2,34},{34,66},{66,9... | collective-permute-start | bytes 172040 | tf_op jit(solution)/shard_map/ppermute | solution.py:17
  79.0 2.9 %collective-permute-done = f32[112,128]{1,0:T(8,128)S(1)} collective-permute-done((f32[112,128]{1,0:T(8,128)S(1)}, f32[112,128]{1,0:T(8,128)S(1)}, u32[]{:S(2)}, u32[]{:S(2)}) %collective-permute-start) | collective-permute-done | bytes 57376 | tf_op jit(solution)/shard_map/ppermute | solution.py:17
  81.8 6.0 %while.101 = (s32[]{:T(128)}, f32[112,128]{1,0:T(8,128)S(1)}, f32[2,112,128]{2,1,0:T(8,128)S(1)}, bf16[2,112,112,128]{3,2,1,0:T(8,128)(2,1)}, s32[]{:T(128)}) while((s32[]{:T(128)}, f32[112,128]{1,0:T(8,128)S(1)}, f32[2,112,128]{2,1,0:T(8,128)S(1)}, bf16[2,112,112,128]{3,2,1,0:T(8,128)(2,1)}, s32[]{:T(128)}) %tuple.213), condition=%wide.region_3.4_spmd, body=%wide.region_2.3_spmd.sunk | while | flops 4816898 | bytes 3498053 | solution.py:31
  81.8 3.0 %multiply_reduce_fusion.24 = f32[128,112]{0,1:T(8,128)S(1)} fusion(f32[128,112]{0,1:T(8,128)S(1)} %bitcast.392, bf16[2,112,112,128]{3,2,1,0:T(8,128)(2,1)} %get-tuple-element.901, s32[]{:T(128)} %get-tuple-element.893), kind=kLoop, calls=%fused_computation.clone.1 | loop fusion | flops 4802560 | bytes 3325956 | tf_op jit(solution)/shard_map/while/body/eval_jaxpr/abl,bl->al/dot_general | solution.py:21
  84.9 3.0 %multiply_reduce_fusion.24 = f32[128,112]{0,1:T(8,128)S(1)} fusion(f32[128,112]{0,1:T(8,128)S(1)} %bitcast.392, bf16[2,112,112,128]{3,2,1,0:T(8,128)(2,1)} %get-tuple-element.901, s32[]{:T(128)} %get-tuple-element.893), kind=kLoop, calls=%fused_computation.clone.1 | loop fusion | flops 4802560 | bytes 3325956 | tf_op jit(solution)/shard_map/while/body/eval_jaxpr/abl,bl->al/dot_general | solution.py:21
  87.9 3.2 %collective-permute-start.1 = (f32[112,128]{1,0:T(8,128)S(1)}, f32[112,128]{1,0:T(8,128)S(1)}, u32[]{:S(2)}, u32[]{:S(2)}) collective-permute-start(f32[112,128]{1,0:T(8,128)S(1)} %get-tuple-element.530), channel_id=1, source_target_pairs={{0,32},{32,64},{64,96},{1,33},{33,65},{65,97},{2,34},{34,66},{66,9... | collective-permute-start | bytes 172040 | tf_op jit(solution)/shard_map/ppermute | solution.py:17
  91.1 2.9 %collective-permute-done.1 = f32[112,128]{1,0:T(8,128)S(1)} collective-permute-done((f32[112,128]{1,0:T(8,128)S(1)}, f32[112,128]{1,0:T(8,128)S(1)}, u32[]{:S(2)}, u32[]{:S(2)}) %collective-permute-start.1) | collective-permute-done | bytes 57376 | tf_op jit(solution)/shard_map/ppermute | solution.py:17
  94.0 6.0 %while.102 = (s32[]{:T(128)}, f32[112,128]{1,0:T(8,128)S(1)}, f32[2,112,128]{2,1,0:T(8,128)S(1)}, bf16[2,112,112,128]{3,2,1,0:T(8,128)(2,1)}, s32[]{:T(128)}) while((s32[]{:T(128)}, f32[112,128]{1,0:T(8,128)S(1)}, f32[2,112,128]{2,1,0:T(8,128)S(1)}, bf16[2,112,112,128]{3,2,1,0:T(8,128)(2,1)}, s32[]{:T(128)}) %tuple.214), condition=%wide.region_5.6_spmd, body=%wide.region_4.5_spmd.sunk | while | flops 4816898 | bytes 3498053 | solution.py:31
  94.0 3.0 %multiply_reduce_fusion.25 = f32[128,112]{0,1:T(8,128)S(1)} fusion(f32[128,112]{0,1:T(8,128)S(1)} %bitcast.393, bf16[2,112,112,128]{3,2,1,0:T(8,128)(2,1)} %get-tuple-element.916, s32[]{:T(128)} %get-tuple-element.908), kind=kLoop, calls=%fused_computation.2.clone.1 | loop fusion | flops 4802560 | bytes 3325956 | tf_op jit(solution)/shard_map/while/body/eval_jaxpr/abl,bl->al/dot_general | solution.py:21
  97.0 3.0 %multiply_reduce_fusion.25 = f32[128,112]{0,1:T(8,128)S(1)} fusion(f32[128,112]{0,1:T(8,128)S(1)} %bitcast.393, bf16[2,112,112,128]{3,2,1,0:T(8,128)(2,1)} %get-tuple-element.916, s32[]{:T(128)} %get-tuple-element.908), kind=kLoop, calls=%fused_computation.2.clone.1 | loop fusion | flops 4802560 | bytes 3325956 | tf_op jit(solution)/shard_map/while/body/eval_jaxpr/abl,bl->al/dot_general | solution.py:21
  100.0 3.4 %collective-permute-start.2 = (f32[112,128]{1,0:T(8,128)S(1)}, f32[112,128]{1,0:T(8,128)S(1)}, u32[]{:S(2)}, u32[]{:S(2)}) collective-permute-start(f32[112,128]{1,0:T(8,128)S(1)} %get-tuple-element.531), channel_id=1, source_target_pairs={{0,32},{32,64},{64,96},{1,33},{33,65},{65,97},{2,34},{34,66},{66,9... | collective-permute-start | bytes 172040 | tf_op jit(solution)/shard_map/ppermute | solution.py:17
  103.4 2.7 %collective-permute-done.2 = f32[112,128]{1,0:T(8,128)S(1)} collective-permute-done((f32[112,128]{1,0:T(8,128)S(1)}, f32[112,128]{1,0:T(8,128)S(1)}, u32[]{:S(2)}, u32[]{:S(2)}) %collective-permute-start.2) | collective-permute-done | bytes 57376 | tf_op jit(solution)/shard_map/ppermute | solution.py:17
  106.1 6.1 %while.103 = (s32[]{:T(128)}, f32[112,128]{1,0:T(8,128)S(1)}, f32[2,112,128]{2,1,0:T(8,128)S(1)}, f32[2,112,128]{2,1,0:T(8,128)S(1)}, bf16[2,112,112,128]{3,2,1,0:T(8,128)(2,1)}, /*index=5*/s32[]{:T(128)}) while((s32[]{:T(128)}, f32[112,128]{1,0:T(8,128)S(1)}, f32[2,112,128]{2,1,0:T(8,128)S(1)}, f32[2,112,128]{2,1,0:T(8,128)S(1)}, ...), condition=%wide.region_7.8_spmd, body=%wide.region_6.7_spmd.sunk | while | flops 4816898 | bytes 3555405 | solution.py:31
  106.1 3.0 %multiply_reduce_fusion.26 = f32[128,112]{0,1:T(8,128)S(1)} fusion(f32[128,112]{0,1:T(8,128)S(1)} %bitcast.391, bf16[2,112,112,128]{3,2,1,0:T(8,128)(2,1)} %get-tuple-element.934, s32[]{:T(128)} %get-tuple-element.924), kind=kLoop, calls=%fused_computation.4.clone.1 | loop fusion | flops 4802560 | bytes 3325956 | tf_op jit(solution)/shard_map/while/body/eval_jaxpr/abl,bl->al/dot_general | solution.py:21
  109.1 3.0 %multiply_reduce_fusion.26 = f32[128,112]{0,1:T(8,128)S(1)} fusion(f32[128,112]{0,1:T(8,128)S(1)} %bitcast.391, bf16[2,112,112,128]{3,2,1,0:T(8,128)(2,1)} %get-tuple-element.934, s32[]{:T(128)} %get-tuple-element.924), kind=kLoop, calls=%fused_computation.4.clone.1 | loop fusion | flops 4802560 | bytes 3325956 | tf_op jit(solution)/shard_map/while/body/eval_jaxpr/abl,bl->al/dot_general | solution.py:21
  112.2 12.4 %while.104 = (s32[]{:T(128)}, f32[112,128]{0,1:T(8,128)S(1)}, f32[2,112,128]{2,1,0:T(8,128)S(1)}, bf16[2,112,112,128]{3,2,1,0:T(8,128)(2,1)}, bf16[2,112,112,128]{3,2,1,0:T(8,128)(2,1)}, /*index=5*/s32[]{:T(128)}) while((s32[]{:T(128)}, f32[112,128]{0,1:T(8,128)S(1)}, f32[2,112,128]{2,1,0:T(8,128)S(1)}, bf16[2,112,112,128]{3,2,1,0:T(8,128)(2,1)}, ...), condition=%wide.region_9.10_spmd, body=%wide.region_8.9_spmd.sunk | while | flops 9619459 | bytes 7053405 | solution.py:41
  112.3 3.0 %multiply_reduce_fusion.27 = f32[128,112]{0,1:T(8,128)S(1)} fusion(f32[128,112]{0,1:T(8,128)S(1)} %copy.151, bf16[2,112,112,128]{3,2,1,0:T(8,128)(2,1)} %get-tuple-element.951, s32[]{:T(128)S(6)} %sub.115), kind=kLoop, calls=%fused_computation.8.clone.1 | loop fusion | flops 4802560 | bytes 3325956 | tf_op jit(solution)/shard_map/while/body/eval_jaxpr/abl,bl->al/dot_general | solution.py:21
  115.3 3.0 %multiply_reduce_fusion.28 = f32[128,112]{0,1:T(8,128)S(1)} fusion(f32[128,112]{0,1:T(8,128)S(1)} %fusion.24, bf16[2,112,112,128]{3,2,1,0:T(8,128)(2,1)} %get-tuple-element.952, s32[]{:T(128)S(6)} %sub.115), kind=kLoop, calls=%fused_computation.7.clone.1 | loop fusion | flops 4802560 | bytes 3325956 | tf_op jit(solution)/shard_map/while
  118.5 3.0 %multiply_reduce_fusion.27 = f32[128,112]{0,1:T(8,128)S(1)} fusion(f32[128,112]{0,1:T(8,128)S(1)} %copy.151, bf16[2,112,112,128]{3,2,1,0:T(8,128)(2,1)} %get-tuple-element.951, s32[]{:T(128)S(6)} %sub.115), kind=kLoop, calls=%fused_computation.8.clone.1 | loop fusion | flops 4802560 | bytes 3325956 | tf_op jit(solution)/shard_map/while/body/eval_jaxpr/abl,bl->al/dot_general | solution.py:21
  121.5 3.0 %multiply_reduce_fusion.28 = f32[128,112]{0,1:T(8,128)S(1)} fusion(f32[128,112]{0,1:T(8,128)S(1)} %fusion.24, bf16[2,112,112,128]{3,2,1,0:T(8,128)(2,1)} %get-tuple-element.952, s32[]{:T(128)S(6)} %sub.115), kind=kLoop, calls=%fused_computation.7.clone.1 | loop fusion | flops 4802560 | bytes 3325956 | tf_op jit(solution)/shard_map/while
  124.6 2.4 %collective-permute-start.3 = (f32[112,128]{0,1:T(8,128)S(1)}, f32[112,128]{0,1:T(8,128)S(1)}, u32[]{:S(2)}, u32[]{:S(2)}) collective-permute-start(f32[112,128]{0,1:T(8,128)S(1)} %get-tuple-element.533), channel_id=1, source_target_pairs={{32,0},{64,32},{96,64},{33,1},{65,33},{97,65},{34,2},{66,34},{98,6... | collective-permute-start | bytes 172040 | tf_op jit(solution)/shard_map/ppermute | solution.py:17
  127.0 3.8 %collective-permute-done.3 = f32[112,128]{0,1:T(8,128)S(1)} collective-permute-done((f32[112,128]{0,1:T(8,128)S(1)}, f32[112,128]{0,1:T(8,128)S(1)}, u32[]{:S(2)}, u32[]{:S(2)}) %collective-permute-start.3) | collective-permute-done | bytes 57376 | tf_op jit(solution)/shard_map/ppermute | solution.py:17
  130.7 12.4 %while.105 = (s32[]{:T(128)}, f32[112,128]{0,1:T(8,128)S(1)}, f32[2,112,128]{2,1,0:T(8,128)S(1)}, bf16[2,112,112,128]{3,2,1,0:T(8,128)(2,1)}, bf16[2,112,112,128]{3,2,1,0:T(8,128)(2,1)}, /*index=5*/s32[]{:T(128)}) while((s32[]{:T(128)}, f32[112,128]{0,1:T(8,128)S(1)}, f32[2,112,128]{2,1,0:T(8,128)S(1)}, ...), condition=%wide.region_11.12_spmd, body=%wide.region_10.11_spmd.sunk | while | flops 9619459 | bytes 7053405 | solution.py:41
  130.8 3.0 %multiply_reduce_fusion.29 = f32[128,112]{0,1:T(8,128)S(1)} fusion(f32[128,112]{0,1:T(8,128)S(1)} %copy.153, bf16[2,112,112,128]{3,2,1,0:T(8,128)(2,1)} %get-tuple-element.969, s32[]{:T(128)S(6)} %sub.117), kind=kLoop, calls=%fused_computation.12.clone.1 | loop fusion | flops 4802560 | bytes 3325956 | tf_op jit(solution)/shard_map/while/body/eval_jaxpr/abl,bl->al/dot_general | solution.py:21
  133.8 3.0 %multiply_reduce_fusion.30 = f32[128,112]{0,1:T(8,128)S(1)} fusion(f32[128,112]{0,1:T(8,128)S(1)} %fusion.25, bf16[2,112,112,128]{3,2,1,0:T(8,128)(2,1)} %get-tuple-element.970, s32[]{:T(128)S(6)} %sub.117), kind=kLoop, calls=%fused_computation.11.clone.1 | loop fusion | flops 4802560 | bytes 3325956 | tf_op jit(solution)/shard_map/while
  137.0 3.0 %multiply_reduce_fusion.29 = f32[128,112]{0,1:T(8,128)S(1)} fusion(f32[128,112]{0,1:T(8,128)S(1)} %copy.153, bf16[2,112,112,128]{3,2,1,0:T(8,128)(2,1)} %get-tuple-element.969, s32[]{:T(128)S(6)} %sub.117), kind=kLoop, calls=%fused_computation.12.clone.1 | loop fusion | flops 4802560 | bytes 3325956 | tf_op jit(solution)/shard_map/while/body/eval_jaxpr/abl,bl->al/dot_general | solution.py:21
  140.1 3.0 %multiply_reduce_fusion.30 = f32[128,112]{0,1:T(8,128)S(1)} fusion(f32[128,112]{0,1:T(8,128)S(1)} %fusion.25, bf16[2,112,112,128]{3,2,1,0:T(8,128)(2,1)} %get-tuple-element.970, s32[]{:T(128)S(6)} %sub.117), kind=kLoop, calls=%fused_computation.11.clone.1 | loop fusion | flops 4802560 | bytes 3325956 | tf_op jit(solution)/shard_map/while
  143.1 2.4 %collective-permute-start.4 = (f32[112,128]{0,1:T(8,128)S(1)}, f32[112,128]{0,1:T(8,128)S(1)}, u32[]{:S(2)}, u32[]{:S(2)}) collective-permute-start(f32[112,128]{0,1:T(8,128)S(1)} %get-tuple-element.534), channel_id=1, source_target_pairs={{32,0},{64,32},{96,64},{33,1},{65,33},{97,65},{34,2},{66,34},{98,6... | collective-permute-start | bytes 172040 | tf_op jit(solution)/shard_map/ppermute | solution.py:17
  145.5 3.8 %collective-permute-done.4 = f32[112,128]{0,1:T(8,128)S(1)} collective-permute-done((f32[112,128]{0,1:T(8,128)S(1)}, f32[112,128]{0,1:T(8,128)S(1)}, u32[]{:S(2)}, u32[]{:S(2)}) %collective-permute-start.4) | collective-permute-done | bytes 57376 | tf_op jit(solution)/shard_map/ppermute | solution.py:17
  149.3 12.4 %while.106 = (s32[]{:T(128)}, f32[112,128]{0,1:T(8,128)S(1)}, f32[2,112,128]{2,1,0:T(8,128)S(1)}, bf16[2,112,112,128]{3,2,1,0:T(8,128)(2,1)}, bf16[2,112,112,128]{3,2,1,0:T(8,128)(2,1)}, /*index=5*/s32[]{:T(128)}) while((s32[]{:T(128)}, f32[112,128]{0,1:T(8,128)S(1)}, f32[2,112,128]{2,1,0:T(8,128)S(1)}, ...), condition=%wide.region_13.14_spmd, body=%wide.region_12.13_spmd.sunk | while | flops 9619459 | bytes 7053405 | solution.py:41
  149.4 3.0 %multiply_reduce_fusion.31 = f32[128,112]{0,1:T(8,128)S(1)} fusion(f32[128,112]{0,1:T(8,128)S(1)} %copy.155, bf16[2,112,112,128]{3,2,1,0:T(8,128)(2,1)} %get-tuple-element.987, s32[]{:T(128)S(6)} %sub.119), kind=kLoop, calls=%fused_computation.16.clone.1 | loop fusion | flops 4802560 | bytes 3325956 | tf_op jit(solution)/shard_map/while/body/eval_jaxpr/abl,bl->al/dot_general | solution.py:21
  152.4 3.0 %multiply_reduce_fusion.32 = f32[128,112]{0,1:T(8,128)S(1)} fusion(f32[128,112]{0,1:T(8,128)S(1)} %fusion.26, bf16[2,112,112,128]{3,2,1,0:T(8,128)(2,1)} %get-tuple-element.988, s32[]{:T(128)S(6)} %sub.119), kind=kLoop, calls=%fused_computation.15.clone.1 | loop fusion | flops 4802560 | bytes 3325956 | tf_op jit(solution)/shard_map/while
  155.6 3.0 %multiply_reduce_fusion.31 = f32[128,112]{0,1:T(8,128)S(1)} fusion(f32[128,112]{0,1:T(8,128)S(1)} %copy.155, bf16[2,112,112,128]{3,2,1,0:T(8,128)(2,1)} %get-tuple-element.987, s32[]{:T(128)S(6)} %sub.119), kind=kLoop, calls=%fused_computation.16.clone.1 | loop fusion | flops 4802560 | bytes 3325956 | tf_op jit(solution)/shard_map/while/body/eval_jaxpr/abl,bl->al/dot_general | solution.py:21
  158.6 3.0 %multiply_reduce_fusion.32 = f32[128,112]{0,1:T(8,128)S(1)} fusion(f32[128,112]{0,1:T(8,128)S(1)} %fusion.26, bf16[2,112,112,128]{3,2,1,0:T(8,128)(2,1)} %get-tuple-element.988, s32[]{:T(128)S(6)} %sub.119), kind=kLoop, calls=%fused_computation.15.clone.1 | loop fusion | flops 4802560 | bytes 3325956 | tf_op jit(solution)/shard_map/while
  161.8 2.4 %collective-permute-start.5 = (f32[112,128]{1,0:T(8,128)S(1)}, f32[112,128]{1,0:T(8,128)S(1)}, u32[]{:S(2)}, u32[]{:S(2)}) collective-permute-start(f32[112,128]{1,0:T(8,128)S(1)} %copy.45), channel_id=1, source_target_pairs={{32,0},{64,32},{96,64},{33,1},{65,33},{97,65},{34,2},{66,34},{98,6... | collective-permute-start | bytes 172040 | tf_op jit(solution)/shard_map/ppermute | solution.py:17
  164.2 3.7 %collective-permute-done.5 = f32[112,128]{1,0:T(8,128)S(1)} collective-permute-done((f32[112,128]{1,0:T(8,128)S(1)}, f32[112,128]{1,0:T(8,128)S(1)}, u32[]{:S(2)}, u32[]{:S(2)}) %collective-permute-start.5) | collective-permute-done | bytes 57376 | tf_op jit(solution)/shard_map/ppermute | solution.py:17
  167.9 12.1 %while.107 = (s32[]{:T(128)}, f32[112,128]{1,0:T(8,128)S(1)}, f32[2,112,128]{2,1,0:T(8,128)S(1)}, f32[2,112,128]{2,1,0:T(8,128)S(1)}, bf16[2,112,112,128]{3,2,1,...) while((s32[]{:T(128)}, f32[112,128]{1,0:T(8,128)S(1)}, f32[2,112,128]{2,1,0:T(8,128)S(1)}, ...), condition=%wide.region_15.16_spmd, body=%wide.region_14.15_spmd.sunk | while | flops 9619459 | bytes 6938729 | solution.py:41
  167.9 3.0 %multiply_reduce_fusion.33 = f32[128,112]{0,1:T(8,128)S(1)} fusion(f32[128,112]{0,1:T(8,128)S(1)} %bitcast.383, bf16[2,112,112,128]{3,2,1,0:T(8,128)(2,1)} %get-tuple-element.1008, s32[]{:T(128)S(6)} %sub.121), kind=kLoop, calls=%fused_computation.20.clone.1 | loop fusion | flops 4802560 | bytes 3325956 | tf_op jit(solution)/shard_map/while/body/eval_jaxpr/abl,bl->al/dot_general | solution.py:21
  170.9 3.0 %multiply_reduce_fusion.34 = f32[128,112]{0,1:T(8,128)S(1)} fusion(f32[128,112]{0,1:T(8,128)S(1)} %fusion.27, bf16[2,112,112,128]{3,2,1,0:T(8,128)(2,1)} %get-tuple-element.1009, s32[]{:T(128)S(6)} %sub.121), kind=kLoop, calls=%fused_computation.19.clone.1 | loop fusion | flops 4802560 | bytes 3325956 | tf_op jit(solution)/shard_map/while/body/eval_jaxpr/abl,bl->al/dot_general | solution.py:21
  173.9 3.0 %multiply_reduce_fusion.33 = f32[128,112]{0,1:T(8,128)S(1)} fusion(f32[128,112]{0,1:T(8,128)S(1)} %bitcast.383, bf16[2,112,112,128]{3,2,1,0:T(8,128)(2,1)} %get-tuple-element.1008, s32[]{:T(128)S(6)} %sub.121), kind=kLoop, calls=%fused_computation.20.clone.1 | loop fusion | flops 4802560 | bytes 3325956 | tf_op jit(solution)/shard_map/while/body/eval_jaxpr/abl,bl->al/dot_general | solution.py:21
  176.9 3.0 %multiply_reduce_fusion.34 = f32[128,112]{0,1:T(8,128)S(1)} fusion(f32[128,112]{0,1:T(8,128)S(1)} %fusion.27, bf16[2,112,112,128]{3,2,1,0:T(8,128)(2,1)} %get-tuple-element.1009, s32[]{:T(128)S(6)} %sub.121), kind=kLoop, calls=%fused_computation.19.clone.1 | loop fusion | flops 4802560 | bytes 3325956 | tf_op jit(solution)/shard_map/while/body/eval_jaxpr/abl,bl->al/dot_general | solution.py:21
  180.0 0.6 copy-done.2
  (71 shorter events, 15.3 us)
Async XLA Ops:
  0.0 2.3 %copy-start = (f32[2,112,128]{2,1,0:T(8,128)S(1)}, f32[2,112,128]{2,1,0:T(8,128)}, u32[]{:S(2)}) copy-start(f32[2,112,128]{2,1,0:T(8,128)} %param.29) | copy-start | bytes 344068
  26.3 8.3 %copy-start.4 = (s32[1,32,64]{2,1,0:T(8,128)S(1)}, s32[1,32,64]{2,1,0:T(8,128)}, u32[]{:S(2)}) copy-start(s32[1,32,64]{2,1,0:T(8,128)} %param.32) | copy-start | bytes 24580
  26.3 37.2 %all-to-all-start = ((f32[32,224,1,64]{1,3,2,0:T(8,128)}), f32[32,224,1,64]{1,3,2,0:T(8,128)S(1)}, u32[]{:S(2)}, u32[]{:S(2)}) async-start(f32[32,224,1,64]{1,3,2,0:T(8,128)} %constant_dynamic-update-slice_fusion), calls=%async_computation | async-start | bytes 4194304 | tf_op jit(solution)/shard_map/all_to_all | solution.py:10
  63.5 1.4 copy-start.1
  64.9 2.7 %copy-start.3 = (f32[2,112,128]{2,1,0:T(8,128)S(1)}, f32[2,112,128]{2,1,0:T(8,128)}, u32[]{:S(2)}) copy-start(f32[2,112,128]{2,1,0:T(8,128)} %param.28) | copy-start | bytes 344068
  75.8 6.1 %collective-permute-start = (f32[112,128]{1,0:T(8,128)S(1)}, f32[112,128]{1,0:T(8,128)S(1)}, u32[]{:S(2)}, u32[]{:S(2)}) collective-permute-start(f32[112,128]{1,0:T(8,128)S(1)} %get-tuple-element.529), channel_id=1, source_target_pairs={{0,32},{32,64},{64,96},{1,33},{33,65},{65,97},{2,34},{34,66},{66,9... | collective-permute-start | bytes 172040 | tf_op jit(solution)/shard_map/ppermute | solution.py:17
  87.9 6.1 %collective-permute-start.1 = (f32[112,128]{1,0:T(8,128)S(1)}, f32[112,128]{1,0:T(8,128)S(1)}, u32[]{:S(2)}, u32[]{:S(2)}) collective-permute-start(f32[112,128]{1,0:T(8,128)S(1)} %get-tuple-element.530), channel_id=1, source_target_pairs={{0,32},{32,64},{64,96},{1,33},{33,65},{65,97},{2,34},{34,66},{66,9... | collective-permute-start | bytes 172040 | tf_op jit(solution)/shard_map/ppermute | solution.py:17
  100.0 6.1 %collective-permute-start.2 = (f32[112,128]{1,0:T(8,128)S(1)}, f32[112,128]{1,0:T(8,128)S(1)}, u32[]{:S(2)}, u32[]{:S(2)}) collective-permute-start(f32[112,128]{1,0:T(8,128)S(1)} %get-tuple-element.531), channel_id=1, source_target_pairs={{0,32},{32,64},{64,96},{1,33},{33,65},{65,97},{2,34},{34,66},{66,9... | collective-permute-start | bytes 172040 | tf_op jit(solution)/shard_map/ppermute | solution.py:17
  124.6 6.2 %collective-permute-start.3 = (f32[112,128]{0,1:T(8,128)S(1)}, f32[112,128]{0,1:T(8,128)S(1)}, u32[]{:S(2)}, u32[]{:S(2)}) collective-permute-start(f32[112,128]{0,1:T(8,128)S(1)} %get-tuple-element.533), channel_id=1, source_target_pairs={{32,0},{64,32},{96,64},{33,1},{65,33},{97,65},{34,2},{66,34},{98,6... | collective-permute-start | bytes 172040 | tf_op jit(solution)/shard_map/ppermute | solution.py:17
  143.1 6.2 %collective-permute-start.4 = (f32[112,128]{0,1:T(8,128)S(1)}, f32[112,128]{0,1:T(8,128)S(1)}, u32[]{:S(2)}, u32[]{:S(2)}) collective-permute-start(f32[112,128]{0,1:T(8,128)S(1)} %get-tuple-element.534), channel_id=1, source_target_pairs={{32,0},{64,32},{96,64},{33,1},{65,33},{97,65},{34,2},{66,34},{98,6... | collective-permute-start | bytes 172040 | tf_op jit(solution)/shard_map/ppermute | solution.py:17
  161.8 6.1 %collective-permute-start.5 = (f32[112,128]{1,0:T(8,128)S(1)}, f32[112,128]{1,0:T(8,128)S(1)}, u32[]{:S(2)}, u32[]{:S(2)}) collective-permute-start(f32[112,128]{1,0:T(8,128)S(1)} %copy.45), channel_id=1, source_target_pairs={{32,0},{64,32},{96,64},{33,1},{65,33},{97,65},{34,2},{66,34},{98,6... | collective-permute-start | bytes 172040 | tf_op jit(solution)/shard_map/ppermute | solution.py:17
  180.0 0.6 copy-start.2
